TPU v7x, 32 devices: a whole 2x2x4 slice. The times are simulated.
32 devices in a mesh: ctx: 4 (over x, core), row: 4 (over z), col: 2 (over y).
Axes of the slice: x: 2, y: 2, z: 4, core: 2. Of those that a mesh axis runs over, the one named last changes fastest.
Arguments:
- states: bfloat16 [384, 4096], P('ctx', 'row'), may hold values from -6 to 6
- context: bfloat16 [384, 4096], P('ctx', 'row'), may hold values from -6 to 6
- up_weight: bfloat16 [4096, 8192], P('row', 'col'), may hold values from -0.09375 to 0.09375
- down_weight: bfloat16 [8192, 4096], P('col', 'row'), may hold values from -0.0625 to 0.0625
- cotangent: bfloat16 [384, 4096], P('ctx', 'row'), may hold values from -6 to 6
Outputs:
- latent: bfloat16 [384, 4096], P('ctx', 'row')
- logdet: float32 [384], P(('ctx', 'row'))
- grad_states: bfloat16 [384, 4096], P('ctx', 'row')
- grad_context: bfloat16 [384, 4096], P('ctx', 'row')
- grad_up: float32 [4096, 8192], P('row', 'col')
- grad_down: float32 [8192, 4096], P('col', 'row')
All inputs are finite; a program needn't handle non-finite values.
Results may differ from a plain program's by a relative error of at most 0.024.
Values may be sent and summed in bfloat16 or wider, within the bound.
A program may use at most 192 MiB of HBM per device.

v0:
```python
import jax
import jax.numpy as jnp
from jax import lax
from jax.sharding import PartitionSpec as P


def silu_slope(hidden):
    sigmoid_part = jax.nn.sigmoid(hidden)
    return sigmoid_part * (1.0 + hidden * (1.0 - sigmoid_part))


def collect(row_block):
    return lax.all_gather(row_block, "row", axis=0, tiled=True)


def feature_total(partial_terms):
    return lax.psum(partial_terms.astype(jnp.bfloat16), "col").astype(jnp.float32)


def contract(left_side, right_side, left_dim, right_dim):
    return lax.dot_general(
        left_side,
        right_side,
        (((left_dim,), (right_dim,)), ((), ())),
        preferred_element_type=jnp.float32,
    )


def shards(states, context, up_weight, down_weight, cotangent):
    hidden = lax.psum_scatter(
        jnp.dot(context, up_weight, preferred_element_type=jnp.float32).astype(jnp.bfloat16),
        "row",
        scatter_dimension=0,
        tiled=True,
    ).astype(jnp.float32)
    activations = collect(jax.nn.silu(hidden).astype(jnp.bfloat16))
    output_terms = jnp.dot(activations, down_weight, preferred_element_type=jnp.float32)
    mixed_total = feature_total(output_terms)
    log_scale = jnp.tanh(mixed_total)
    shrink = jnp.exp(-log_scale)
    flowed = states.astype(jnp.float32) * shrink
    cotangent_wide = cotangent.astype(jnp.float32)
    det_terms = -jnp.sum(log_scale, axis=1)
    scale_rows = ((1.0 - cotangent_wide * flowed) * (1.0 - log_scale * log_scale)).astype(
        jnp.bfloat16
    )
    down_part = contract(activations, scale_rows, 0, 0)
    grad_down = lax.psum(down_part.astype(jnp.bfloat16), "ctx").astype(jnp.float32)
    back_terms = contract(scale_rows, down_weight, 1, 1)
    back_rows = lax.psum_scatter(
        back_terms.astype(jnp.bfloat16), "row", scatter_dimension=0, tiled=True
    ).astype(jnp.float32)
    logdet = lax.psum_scatter(det_terms, "row", scatter_dimension=0, tiled=True)
    slope_rows = (back_rows * silu_slope(hidden)).astype(jnp.bfloat16)
    slope_all = collect(slope_rows)
    input_terms = contract(slope_all, up_weight, 1, 1)
    grad_states = (cotangent_wide * shrink).astype(jnp.bfloat16)
    grad_context = feature_total(input_terms).astype(jnp.bfloat16)
    up_part = contract(context, slope_all, 0, 0)
    grad_up = lax.psum(up_part.astype(jnp.bfloat16), "ctx").astype(jnp.float32)
    return (flowed.astype(jnp.bfloat16), logdet, grad_states, grad_context, grad_up, grad_down)


def solution(mesh):
    placed = (P("ctx", "row"), P("ctx", "row"), P("row", "col"), P("col", "row"), P("ctx", "row"))
    return jax.shard_map(
        shards,
        mesh=mesh,
        in_specs=placed,
        out_specs=(
            P("ctx", "row"),
            P(("ctx", "row")),
            P("ctx", "row"),
            P("ctx", "row"),
            P("row", "col"),
            P("col", "row"),
        ),
        check_vma=False,
    )
```

profile of v0, /device:TPU:0, one launch (start us, length us, event | category | flops | bytes accessed | tf_op | source)
XLA Modules:
  0.0 463.3 jit_solution(15541179772895529971)
XLA Ops:
  7.2 0.9 copy-done
  8.1 5.7 %convolution_convert_fusion.2 = bf16[96,4096]{1,0:T(8,128)(2,1)} fusion(bf16[96,1024]{1,0:T(8,128)(2,1)S(1)} %copy-done, bf16[1024,4096]{1,0:T(8,128)(2,1)} %param.7), kind=kOutput, calls=%fused_computation.3 | convolution fusion | flops 805699584 | bytes 9371648 | tf_op jit(solution)/shard_map/dot_general | solution.py:31
  13.9 26.1 %reduce-scatter.3.cloned.1.call-done = bf16[24,4096]{1,0:T(8,128)(2,1)} async-done(((bf16[96,4096]{1,0:T(8,128)(2,1)}), bf16[24,4096]{1,0:T(8,128)(2,1)}) %reduce-scatter.3.cloned.1.call-update) | async-done | bytes 196624 | tf_op jit(solution)/shard_map/reduce_scatter | solution.py:30
  40.0 1.0 fusion.7
  41.0 18.0 %all_gather.6 = bf16[96,4096]{1,0:T(8,128)(2,1)S(1)} all-gather(bf16[24,4096]{1,0:T(8,128)(2,1)S(1)} %fusion.7), channel_id=1, replica_groups=mesh['ctx'=4,'row'=4,'col'=2] {'row'}, dimensions={0}, use_global_device_ids=true | all-gather | bytes 983040 | tf_op jit(solution)/shard_map/all_gather | solution.py:13
  59.0 5.6 %convolution_convert_fusion.4 = bf16[96,1024]{1,0:T(8,128)(2,1)} fusion(bf16[96,4096]{1,0:T(8,128)(2,1)S(1)} %all_gather.6, bf16[4096,1024]{1,0:T(8,128)(2,1)} %param.8), kind=kOutput, calls=%fused_computation.5 | convolution fusion | flops 805404672 | bytes 9371648 | tf_op jit(solution)/shard_map/dot_general | solution.py:37
  64.7 21.7 %all-reduce.6.cloned.1.call-done = bf16[96,1024]{1,0:T(8,128)(2,1)} async-done(((bf16[96,1024]{1,0:T(8,128)(2,1)}), bf16[96,1024]{1,0:T(8,128)(2,1)}) %all-reduce.6.cloned.1.call-update) | async-done | bytes 196624 | tf_op jit(solution)/shard_map/psum | solution.py:17
  86.4 7.1 %convolution_convert_fusion.1 = bf16[96,4096]{1,0:T(8,128)(2,1)} fusion(bf16[4096,1024]{1,0:T(8,128)(2,1)} %param.8, bf16[96,1024]{1,0:T(8,128)(2,1)S(1)} %copy-done.2, bf16[96,1024]{1,0:T(8,128)(2,1)} %all-reduce.6.cloned.1.call-done, bf16[96,1024]{1,0:T(8,128)(2,1)S(1)} %copy-done.3), kind=kOutput, calls=%fused_computation.2 | convolution fusion | flops 806780928 | bytes 9764864 | tf_op jit(solution)/shard_map/dot_general | solution.py:21
  93.6 5.8 %convolution_convert_fusion = bf16[4096,1024]{1,0:T(8,128)(2,1)} fusion(bf16[96,4096]{1,0:T(8,128)(2,1)S(1)} %all_gather.6, bf16[96,1024]{1,0:T(8,128)(2,1)S(1)} %copy-done.2, bf16[96,1024]{1,0:T(8,128)(2,1)S(1)} %copy-done.4, bf16[96,1024]{1,0:T(8,128)(2,1)S(1)} %copy-done.3), kind=kOutput, calls=%fused_computation.1 | convolution fusion | flops 810582016 | bytes 9764864 | tf_op jit(solution)/shard_map/dot_general | solution.py:21
  99.4 17.6 %reduce-scatter.5.cloned.1.call-done = bf16[24,4096]{1,0:T(8,128)(2,1)} async-done(((bf16[96,4096]{1,0:T(8,128)(2,1)}), bf16[24,4096]{1,0:T(8,128)(2,1)}) %reduce-scatter.5.cloned.1.call-update) | async-done | bytes 196624 | tf_op jit(solution)/shard_map/reduce_scatter | solution.py:50
  117.0 1.1 fusion.11
  118.1 17.9 %all_gather.7 = bf16[96,4096]{1,0:T(8,128)(2,1)S(1)} all-gather(bf16[24,4096]{1,0:T(8,128)(2,1)S(1)} %fusion.11), channel_id=1, replica_groups=mesh['ctx'=4,'row'=4,'col'=2] {'row'}, dimensions={0}, use_global_device_ids=true | all-gather | bytes 983040 | tf_op jit(solution)/shard_map/all_gather | solution.py:13
  136.1 5.8 %convert_bitcast_fusion = bf16[1024,4096]{0,1:T(8,128)(2,1)} fusion(bf16[96,4096]{1,0:T(8,128)(2,1)S(1)} %all_gather.7, bf16[96,1024]{1,0:T(8,128)(2,1)S(1)} %copy-done), kind=kOutput, calls=%fused_computation | convolution fusion | flops 809500672 | bytes 9371648 | tf_op jit(solution)/shard_map/dot_general | solution.py:21
  142.1 0.4 copy-done.6
  142.5 0.6 dynamic-slice
  143.7 7.2 %convolution_convert_fusion.3 = bf16[96,1024]{1,0:T(8,128)(2,1)} fusion(bf16[96,4096]{1,0:T(8,128)(2,1)S(1)} %all_gather.7, bf16[1024,4096]{1,0:T(8,128)(2,1)} %param.7), kind=kOutput, calls=%fused_computation.4 | convolution fusion | flops 805404672 | bytes 9371648 | tf_op jit(solution)/shard_map/dot_general | solution.py:21
  151.0 1.0 fusion
  152.0 9.6 %all-reduce = f32[96]{0:T(128)S(1)} all-reduce(f32[96]{0:T(128)S(1)} %neg.13), channel_id=3, replica_groups=mesh['ctx'=4,'row'=4,'col'=2] {'row'}, use_global_device_ids=true, to_apply=%region_3.4.clone | all-reduce | flops 96 | bytes 768
  161.6 0.6 dynamic-slice.1
  162.2 268.0 %all-reduce.10.cloned.1.call-done = (bf16[1024,4096]{0,1:T(8,128)(2,1)}, bf16[4096,1024]{1,0:T(8,128)(2,1)}) async-done(((bf16[1024,4096]{0,1:T(8,128)(2,1)}, bf16[4096,1024]{1,0:T(8,128)(2,1)}), (bf16[1024,4096]{0,1:T(8,128)(2,1)}, bf16[4096,1024]{1,0:T(8,128)(2,1)})) %all-reduce.10.cloned.1.call-update) | async-done | bytes 16777232 | tf_op jit(solution)/shard_map/psum | solution.py:60
  430.1 12.3 %copy.12 = f32[1024,4096]{1,0:T(8,128)} copy(bf16[1024,4096]{0,1:T(8,128)(2,1)} %get-tuple-element.18) | data formatting | bytes 25165824
  442.5 11.8 %convert_element_type.77 = f32[4096,1024]{1,0:T(8,128)} convert(bf16[4096,1024]{1,0:T(8,128)(2,1)} %get-tuple-element.19) | non-fusion elementwise | flops 4194304 | bytes 25165824 | tf_op jit(solution)/shard_map/convert_element_type | solution.py:48
  454.2 1.0 all-reduce.8.cloned.1.call-done
  455.2 1.6 copy.17
  (23 shorter events, 0.5 us)
Async XLA Ops:
  7.2 0.9 copy-start
  7.2 32.8 %reduce-scatter.3.cloned.1.call-start = ((), (), s32[]{:S(2)}) async-start(), calls=%async_computation.2 | async-start | bytes 983040 | tf_op jit(solution)/shard_map/reduce_scatter | solution.py:30
  13.8 72.5 %all-reduce.6.cloned.1.call-start = ((), (), s32[]{:S(2)}) async-start(), calls=%async_computation.3 | async-start | bytes 393216 | tf_op jit(solution)/shard_map/psum | solution.py:17
  59.0 27.3 %copy-start.2 = (bf16[96,1024]{1,0:T(8,128)(2,1)S(1)}, bf16[96,1024]{1,0:T(8,128)(2,1)}, u32[]{:S(2)}) copy-start(bf16[96,1024]{1,0:T(8,128)(2,1)} %param.9) | copy-start | bytes 589828
  59.0 27.3 %copy-start.3 = (bf16[96,1024]{1,0:T(8,128)(2,1)S(1)}, bf16[96,1024]{1,0:T(8,128)(2,1)}, u32[]{:S(2)}) copy-start(bf16[96,1024]{1,0:T(8,128)(2,1)} %param.5) | copy-start | bytes 589828
  64.6 52.4 %reduce-scatter.5.cloned.1.call-start = ((), (), s32[]{:S(2)}) async-start(), calls=%async_computation.4 | async-start | bytes 983040 | tf_op jit(solution)/shard_map/reduce_scatter | solution.py:50
  86.4 7.2 %copy-start.4 = (bf16[96,1024]{1,0:T(8,128)(2,1)S(1)}, bf16[96,1024]{1,0:T(8,128)(2,1)}, u32[]{:S(2)}) copy-start(bf16[96,1024]{1,0:T(8,128)(2,1)} %all-reduce.6.cloned.1.call-done) | copy-start | bytes 589828
  93.5 23.5 %copy-start.5 = (bf16[24,4096]{1,0:T(8,128)(2,1)S(1)}, bf16[24,4096]{1,0:T(8,128)(2,1)}, u32[]{:S(2)}) copy-start(bf16[24,4096]{1,0:T(8,128)(2,1)} %reduce-scatter.3.cloned.1.call-done) | copy-start | bytes 589828
  93.5 336.6 %all-reduce.10.cloned.1.call-start = ((), (), s32[]{:S(2)}) async-start(), calls=%async_computation.6 | async-start | bytes 33554432 | tf_op jit(solution)/shard_map/psum | solution.py:60
  141.8 0.7 copy-start.6
  141.9 313.3 %all-reduce.8.cloned.1.call-start = ((), (), s32[]{:S(2)}) async-start(), calls=%async_computation.5 | async-start | bytes 393216 | tf_op jit(solution)/shard_map/psum | solution.py:17
  442.5 14.3 %copy-start.1 = (bf16[96,1024]{1,0:T(8,128)(2,1)S(1)}, bf16[96,1024]{1,0:T(8,128)(2,1)}, u32[]{:S(2)}) copy-start(bf16[96,1024]{1,0:T(8,128)(2,1)} %param.6) | copy-start | bytes 589828
Sparse Core Ops, SparseCore 0:
  14.0 25.9 reduce-scatter.2
  64.7 21.5 all-reduce.5
  93.6 23.3 reduce-scatter.4
  142.0 288.0 all-reduce.9
  432.8 22.3 all-reduce.7
where the time goes:
time: 464 us; the launch traced here: 463 us
  waiting for transfers between devices  334 us (72%)
  blocking collectives  45.5 us (10%)
  matrix products  37.2 us (8%)
  local copies, waits for them, and re-layouts  16.4 us (4%)
  other arithmetic  14.9 us (3%)
  between operations  14.5 us (3%)
    psum x1, waiting for transfers between devices, shards(): grad_up = lax.psum(up_part.astype(jnp.bfloat16), 'ctx').astype(jnp.float32)  268 us
    all_gather x2, blocking collectives, collect(): return lax.all_gather(row_block, 'row', axis=0, tiled=True)  35.9 us
    reduce_scatter x1, waiting for transfers between devices, shards(): lax.psum_scatter(jnp.dot(context, up_weight, preferred_element_type=jnp.f...  26.1 us
    dot_general x4, matrix products, contract(): lax.dot_general(left_side, right_side, (((left_dim,), (right_dim,)), ((),...  25.9 us
    psum x2, waiting for transfers between devices, feature_total(): lax.psum(partial_terms.astype(jnp.bfloat16), 'col').astype(jnp.float32)  22.6 us
    reduce_scatter x1, waiting for transfers between devices, shards(): lax.psum_scatter(back_terms.astype(jnp.bfloat16), 'row', scatter_dimensio...  17.6 us
    unnamed x18, local copies, waits for them, and re-layouts  16.4 us
    convert_element_type x1, other arithmetic, shards(): lax.psum(down_part.astype(jnp.bfloat16), 'ctx').astype(jnp.float32)  11.8 us
  transfers between devices with their start and end apart: 5, of which 5 were waited for; matrix products, arithmetic and copies ran while one was open for 8% of the time, Pallas kernels for 0%

commit v1 on v0

--- a/solution.py
+++ b/solution.py
@@ -14,7 +14,9 @@
 
 
 def feature_total(partial_terms):
-    return lax.psum(partial_terms.astype(jnp.bfloat16), "col").astype(jnp.float32)
+    return jnp.sum(lax.all_gather(partial_terms.astype(jnp.bfloat16), "col"), axis=0).astype(
+        jnp.float32
+    )
 
 
 def contract(left_side, right_side, left_dim, right_dim):

time: 464 us -> 445 us (0.959)
  waiting for transfers between devices: 334 us -> 304 us
  blocking collectives: 45.5 us -> 58.9 us
    psum x2 -> x0, waiting for transfers between devices: 22.6 us -> none  [feature_total(): lax.psum(partial_terms.astype(jnp.bfloat16), 'col').astype(jnp.float32)]
    all_gather x0 -> x2, blocking collectives: none -> 12.7 us  [feature_total(): lax.all_gather(partial_terms.astype(jnp.bfloat16), 'col')]
    psum x1, waiting for transfers between devices: 268 us -> 261 us  [shards(): grad_up = lax.psum(up_part.astype(jnp.bfloat16), 'ctx').astype(jnp.float32)]
    unnamed x18 -> x15, local copies, waits for them, and re-layouts: 16.4 us -> 15 us
  transfers between devices with their start and end apart: 5 -> 3, of which waited for: 5 -> 3; matrix products, arithmetic and copies ran while one was open for 8% -> 3% of each run, Pallas kernels for 0% -> 0%
where the time goes in v1:
time: 445 us; the launch traced here: 444 us
  waiting for transfers between devices  304 us (68%)
  blocking collectives  58.9 us (13%)
  matrix products  35.4 us (8%)
  other arithmetic  15.7 us (4%)
  local copies, waits for them, and re-layouts  15 us (3%)
  between operations  14.5 us (3%)
    psum x1, waiting for transfers between devices, shards(): grad_up = lax.psum(up_part.astype(jnp.bfloat16), 'ctx').astype(jnp.float32)  261 us
    all_gather x2, blocking collectives, collect(): return lax.all_gather(row_block, 'row', axis=0, tiled=True)  36 us
    reduce_scatter x1, waiting for transfers between devices, shards(): lax.psum_scatter(jnp.dot(context, up_weight, preferred_element_type=jnp.f...  26.1 us
    dot_general x4, matrix products, contract(): lax.dot_general(left_side, right_side, (((left_dim,), (right_dim,)), ((),...  24.7 us
    reduce_scatter x1, waiting for transfers between devices, shards(): lax.psum_scatter(back_terms.astype(jnp.bfloat16), 'row', scatter_dimensio...  16.9 us
    unnamed x15, local copies, waits for them, and re-layouts  15 us
    all_gather x2, blocking collectives, feature_total(): lax.all_gather(partial_terms.astype(jnp.bfloat16), 'col')  12.7 us
    convert_element_type x1, other arithmetic, shards(): lax.psum(down_part.astype(jnp.bfloat16), 'ctx').astype(jnp.float32)  11.7 us
  transfers between devices with their start and end apart: 3, of which 3 were waited for; matrix products, arithmetic and copies ran while one was open for 3% of the time, Pallas kernels for 0%

profile of v1, /device:TPU:0, one launch (start us, length us, event | category | flops | bytes accessed | tf_op | source)
XLA Modules:
  0.0 443.9 jit_solution(11038669878883226363)
XLA Ops:
  7.2 0.9 copy-done
  8.1 5.7 %convolution_convert_fusion.2 = bf16[96,4096]{1,0:T(8,128)(2,1)} fusion(bf16[96,1024]{1,0:T(8,128)(2,1)S(1)} %copy-done, bf16[1024,4096]{1,0:T(8,128)(2,1)} %param.7), kind=kOutput, calls=%fused_computation.3 | convolution fusion | flops 805699584 | bytes 9371648 | tf_op jit(solution)/shard_map/dot_general | solution.py:33
  13.9 26.1 %reduce-scatter.3.cloned.1.call-done = bf16[24,4096]{1,0:T(8,128)(2,1)} async-done(((bf16[96,4096]{1,0:T(8,128)(2,1)}), bf16[24,4096]{1,0:T(8,128)(2,1)}) %reduce-scatter.3.cloned.1.call-update) | async-done | bytes 196624 | tf_op jit(solution)/shard_map/reduce_scatter | solution.py:32
  40.0 1.0 fusion.7
  41.0 18.0 %all_gather.18 = bf16[96,4096]{1,0:T(8,128)(2,1)S(1)} all-gather(bf16[24,4096]{1,0:T(8,128)(2,1)S(1)} %fusion.7), channel_id=1, replica_groups=mesh['ctx'=4,'row'=4,'col'=2] {'row'}, dimensions={0}, use_global_device_ids=true | all-gather | bytes 983040 | tf_op jit(solution)/shard_map/all_gather | solution.py:13
  59.0 4.9 %convolution_convert_fusion.4 = bf16[96,1024]{1,0:T(8,128)(2,1)S(1)} fusion(bf16[96,4096]{1,0:T(8,128)(2,1)S(1)} %all_gather.18, bf16[4096,1024]{1,0:T(8,128)(2,1)} %param.8), kind=kOutput, calls=%fused_computation.5 | convolution fusion | flops 805404672 | bytes 9371648 | tf_op jit(solution)/shard_map/dot_general | solution.py:39
  63.9 6.3 %all-gather = bf16[192,1024]{1,0:T(8,128)(2,1)S(1)} all-gather(bf16[96,1024]{1,0:T(8,128)(2,1)S(1)} %convolution_convert_fusion.4), channel_id=2, replica_groups=mesh['ctx'=4,'row'=4,'col'=2] {'col'}, dimensions={0}, use_global_device_ids=true | all-gather | bytes 589824 | tf_op jit(solution)/shard_map/all_gather | solution.py:17
  70.4 7.0 %convolution_convert_fusion.1 = bf16[96,4096]{1,0:T(8,128)(2,1)} fusion(bf16[4096,1024]{1,0:T(8,128)(2,1)} %param.8, bf16[96,1024]{1,0:T(8,128)(2,1)S(1)} %copy-done.2, bf16[96,1024]{1,0:T(8,128)(2,1)S(1)} %reduce_sum.33, bf16[96,1024]{1,0:T(8,128)(2,1)S(1)} %copy-done.3), kind=kOutput, calls=%fused_computation.2 | convolution fusion | flops 806780928 | bytes 9764864 | tf_op jit(solution)/shard_map/dot_general | solution.py:23
  77.4 5.8 %convolution_convert_fusion = bf16[4096,1024]{1,0:T(8,128)(2,1)} fusion(bf16[96,4096]{1,0:T(8,128)(2,1)S(1)} %all_gather.18, bf16[96,1024]{1,0:T(8,128)(2,1)S(1)} %copy-done.2, bf16[96,1024]{1,0:T(8,128)(2,1)S(1)} %reduce_sum.33, bf16[96,1024]{1,0:T(8,128)(2,1)S(1)} %copy-done.3), kind=kOutput, calls=%fused_computation.1 | convolution fusion | flops 810582016 | bytes 9764864 | tf_op jit(solution)/shard_map/dot_general | solution.py:23
  83.2 16.9 %reduce-scatter.5.cloned.1.call-done = bf16[24,4096]{1,0:T(8,128)(2,1)} async-done(((bf16[96,4096]{1,0:T(8,128)(2,1)}), bf16[24,4096]{1,0:T(8,128)(2,1)}) %reduce-scatter.5.cloned.1.call-update) | async-done | bytes 196624 | tf_op jit(solution)/shard_map/reduce_scatter | solution.py:52
  100.1 1.1 fusion.11
  101.2 18.0 %all_gather.21 = bf16[96,4096]{1,0:T(8,128)(2,1)S(1)} all-gather(bf16[24,4096]{1,0:T(8,128)(2,1)S(1)} %fusion.11), channel_id=1, replica_groups=mesh['ctx'=4,'row'=4,'col'=2] {'row'}, dimensions={0}, use_global_device_ids=true | all-gather | bytes 983040 | tf_op jit(solution)/shard_map/all_gather | solution.py:13
  119.2 5.8 %convert_bitcast_fusion = bf16[1024,4096]{0,1:T(8,128)(2,1)} fusion(bf16[96,4096]{1,0:T(8,128)(2,1)S(1)} %all_gather.21, bf16[96,1024]{1,0:T(8,128)(2,1)S(1)} %copy-done), kind=kOutput, calls=%fused_computation | convolution fusion | flops 809500672 | bytes 9371648 | tf_op jit(solution)/shard_map/dot_general | solution.py:23
  125.0 0.6 copy-done.5
  125.6 0.6 dynamic-slice
  126.9 1.0 fusion
  127.9 10.2 %all-reduce = f32[96]{0:T(128)S(1)} all-reduce(f32[96]{0:T(128)S(1)} %neg.13), channel_id=5, replica_groups=mesh['ctx'=4,'row'=4,'col'=2] {'row'}, use_global_device_ids=true, to_apply=%region_3.4.clone | all-reduce | flops 96 | bytes 768
  138.1 0.6 dynamic-slice.1
  138.7 6.2 %convolution_convert_fusion.3 = bf16[96,1024]{1,0:T(8,128)(2,1)S(1)} fusion(bf16[96,4096]{1,0:T(8,128)(2,1)S(1)} %all_gather.21, bf16[1024,4096]{1,0:T(8,128)(2,1)} %param.7), kind=kOutput, calls=%fused_computation.4 | convolution fusion | flops 805404672 | bytes 9371648 | tf_op jit(solution)/shard_map/dot_general | solution.py:23
  144.9 6.3 %all-gather.1 = bf16[192,1024]{1,0:T(8,128)(2,1)S(1)} all-gather(bf16[96,1024]{1,0:T(8,128)(2,1)S(1)} %convolution_convert_fusion.3), channel_id=3, replica_groups=mesh['ctx'=4,'row'=4,'col'=2] {'col'}, dimensions={0}, use_global_device_ids=true | all-gather | bytes 589824 | tf_op jit(solution)/shard_map/all_gather | solution.py:17
  151.2 0.8 reduce_sum.35
  152.0 261.2 %all-reduce.4.cloned.1.call-done = (bf16[1024,4096]{0,1:T(8,128)(2,1)}, bf16[4096,1024]{1,0:T(8,128)(2,1)}) async-done(((bf16[1024,4096]{0,1:T(8,128)(2,1)}, bf16[4096,1024]{1,0:T(8,128)(2,1)}), (bf16[1024,4096]{0,1:T(8,128)(2,1)}, bf16[4096,1024]{1,0:T(8,128)(2,1)})) %all-reduce.4.cloned.1.call-update) | async-done | bytes 16777232 | tf_op jit(solution)/shard_map/psum | solution.py:62
  413.3 12.3 %copy.12 = f32[1024,4096]{1,0:T(8,128)} copy(bf16[1024,4096]{0,1:T(8,128)(2,1)} %get-tuple-element.18) | data formatting | bytes 25165824
  425.6 11.7 %convert_element_type.81 = f32[4096,1024]{1,0:T(8,128)} convert(bf16[4096,1024]{1,0:T(8,128)(2,1)} %get-tuple-element.19) | non-fusion elementwise | flops 4194304 | bytes 25165824 | tf_op jit(solution)/shard_map/convert_element_type | solution.py:50
  (18 shorter events, 0.3 us)
Async XLA Ops:
  7.2 0.9 copy-start
  7.2 32.8 %reduce-scatter.3.cloned.1.call-start = ((), (), s32[]{:S(2)}) async-start(), calls=%async_computation.2 | async-start | bytes 983040 | tf_op jit(solution)/shard_map/reduce_scatter | solution.py:32
  13.8 86.3 %reduce-scatter.5.cloned.1.call-start = ((), (), s32[]{:S(2)}) async-start(), calls=%async_computation.3 | async-start | bytes 983040 | tf_op jit(solution)/shard_map/reduce_scatter | solution.py:52
  59.0 11.3 %copy-start.2 = (bf16[96,1024]{1,0:T(8,128)(2,1)S(1)}, bf16[96,1024]{1,0:T(8,128)(2,1)}, u32[]{:S(2)}) copy-start(bf16[96,1024]{1,0:T(8,128)(2,1)} %param.9) | copy-start | bytes 589828
  59.0 11.3 %copy-start.3 = (bf16[96,1024]{1,0:T(8,128)(2,1)S(1)}, bf16[96,1024]{1,0:T(8,128)(2,1)}, u32[]{:S(2)}) copy-start(bf16[96,1024]{1,0:T(8,128)(2,1)} %param.5) | copy-start | bytes 589828
  77.3 22.8 %copy-start.4 = (bf16[24,4096]{1,0:T(8,128)(2,1)S(1)}, bf16[24,4096]{1,0:T(8,128)(2,1)}, u32[]{:S(2)}) copy-start(bf16[24,4096]{1,0:T(8,128)(2,1)} %reduce-scatter.3.cloned.1.call-done) | copy-start | bytes 589828
  77.4 335.9 %all-reduce.4.cloned.1.call-start = ((), (), s32[]{:S(2)}) async-start(), calls=%async_computation.4 | async-start | bytes 33554432 | tf_op jit(solution)/shard_map/psum | solution.py:62
  125.0 0.7 copy-start.5
  425.6 11.7 %copy-start.1 = (bf16[96,1024]{1,0:T(8,128)(2,1)S(1)}, bf16[96,1024]{1,0:T(8,128)(2,1)}, u32[]{:S(2)}) copy-start(bf16[96,1024]{1,0:T(8,128)(2,1)} %param.6) | copy-start | bytes 589828
Sparse Core Ops, SparseCore 0:
  14.0 25.9 reduce-scatter.2
  77.5 22.5 reduce-scatter.4
  125.1 288.0 all-reduce.3
